TPU v7x, 32 devices: a whole 2x2x4 slice. The times are simulated.
32 devices in a mesh: depth: 8 (over z, y), lat: 4 (over x, core).
Axes of the slice: x: 2, y: 2, z: 4, core: 2. Of those that a mesh axis runs over, the one named last changes fastest.
Arguments:
- object_slices: float32 [8, 2, 512, 2048], P('depth', None, 'lat'), as said below
- probe: float32 [2, 2, 256, 256], replicated, may hold values from -2.7 to 2.7
- positions: int32 [16, 2], P('lat'), may hold values from 0 to 1792, as said below
- measured: float32 [16, 256, 256], P('lat'), may hold values from 0 to 0.8
Outputs:
- object_grad: float32 [8, 2, 512, 2048], P('depth', None, 'lat')
Inputs may be any that keep to these rules, and one draw needn't show every extreme that they name: Rows 4 l ... 4 l + 3 are the positions of lat index l: their row offset lies in [l * 128, (l + 1) * 128) and their column offset in [0, 1792]. `object_slices`: each cell's magnitude, sqrt(real part squared plus imaginary part squared), lies between 0.9 and 1.
All inputs are finite; a program needn't handle non-finite values.
Results may differ from a plain program's by a relative error of at most 0.039.
Values may be sent and summed in bfloat16 or wider, within the bound.
A program may use at most 64 MiB of HBM per device.

v0:
```python
import math

import jax
import jax.numpy as jnp
from jax import lax
from jax.sharding import PartitionSpec as P

fresnel = 0.5


def shifted(block, axis, distance):
    devices = range(lax.axis_size(axis))
    route = [((i - distance) % len(devices), i) for i in devices]
    return lax.ppermute(block, axis, route)


def from_behind(block, axis, distance):
    devices = range(lax.axis_size(axis))
    route = [(i - distance, i) for i in devices if i - distance in devices]
    return lax.ppermute(block, axis, route)


def stack_block(real_part, imag_part):
    return jnp.stack([jnp.stack([real_part, -imag_part]), jnp.stack([imag_part, real_part])])


def make_tables(pixels):
    highest = lax.Precision.HIGHEST
    steps_idx = jnp.arange(pixels, dtype=jnp.int32)
    product = steps_idx[:, None] * steps_idx[None, :] % pixels
    angle = 2.0 * math.pi / pixels * product.astype(jnp.float32)
    scale = 1.0 / math.sqrt(pixels)
    d_real = jnp.cos(angle) * scale
    d_imag = -jnp.sin(angle) * scale
    freq = jnp.where(steps_idx < pixels // 2, steps_idx, steps_idx - pixels).astype(jnp.float32)
    theta = math.pi * fresnel / pixels * freq * freq
    h_real = jnp.cos(theta)
    h_imag = -jnp.sin(theta)
    a_real = d_real * h_real[None, :] + d_imag * h_imag[None, :]
    a_imag = d_real * h_imag[None, :] - d_imag * h_real[None, :]
    k_real = jnp.dot(a_real, d_real, precision=highest) - jnp.dot(a_imag, d_imag, precision=highest)
    k_imag = jnp.dot(a_real, d_imag, precision=highest) + jnp.dot(a_imag, d_real, precision=highest)
    return (
        stack_block(k_real, k_imag),
        stack_block(k_real.T, -k_imag.T),
        stack_block(d_real, d_imag),
        stack_block(d_real, -d_imag),
    )


def transform(table, wave):
    highest = lax.Precision.HIGHEST
    middle = jnp.einsum("srij,mrjk->msik", table, wave.astype(jnp.float32), precision=highest)
    return jnp.einsum("mrik,srlk->msil", middle, table, precision=highest)


def multiply(object_patch, wave_in):
    real_part = object_patch[0] * wave_in[:, 0] - object_patch[1] * wave_in[:, 1]
    imag_part = object_patch[0] * wave_in[:, 1] + object_patch[1] * wave_in[:, 0]
    return jnp.stack([real_part, imag_part], axis=1)


def conj_multiply(object_patch, wave_in):
    real_part = object_patch[0] * wave_in[:, 0] + object_patch[1] * wave_in[:, 1]
    imag_part = object_patch[0] * wave_in[:, 1] - object_patch[1] * wave_in[:, 0]
    return jnp.stack([real_part, imag_part], axis=1)


def conj_sum(wave_in, grad_lit):
    real_part = wave_in[:, 0] * grad_lit[:, 0] + wave_in[:, 1] * grad_lit[:, 1]
    imag_part = wave_in[:, 0] * grad_lit[:, 1] - wave_in[:, 1] * grad_lit[:, 0]
    return jnp.stack([jnp.sum(real_part, axis=0), jnp.sum(imag_part, axis=0)])


def on_device(object_slices, probe, positions, measured):
    pixels = probe.shape[-1]
    tile_rows = object_slices.shape[2]
    local_count = positions.shape[0]
    depth_size = lax.axis_size("depth")
    my_section = lax.axis_index("depth")
    prop_table, prop_adjoint, far_table, far_adjoint = make_tables(pixels)
    own_tile = object_slices[0]
    next_tile = shifted(own_tile, "lat", -1)
    after_tile = shifted(next_tile, "lat", -1)
    extended = jnp.concatenate([own_tile, next_tile, after_tile], axis=1)
    start_wave = probe.astype(jnp.bfloat16)
    zero_wave = jnp.zeros(probe.shape, jnp.bfloat16)
    saved_init = jnp.zeros((local_count,) + probe.shape, jnp.bfloat16)
    accum_init = jnp.zeros(extended.shape, jnp.float32)

    def corner(which):
        place = lax.dynamic_index_in_dim(positions, which, 0, False)
        return (place[0] % tile_rows, place[1])

    def forward_work(which, incoming, saved, seeds):
        in_wave = jnp.where(my_section == 0, start_wave, incoming)
        row_start, col_start = corner(which)
        patch_block = lax.dynamic_slice(extended, (0, row_start, col_start), (2, pixels, pixels))
        lit_wave = multiply(patch_block, in_wave.astype(jnp.float32))
        out_wave = transform(prop_table, lit_wave).astype(jnp.bfloat16)
        saved = lax.dynamic_update_index_in_dim(saved, in_wave, which, 0)
        target = lax.dynamic_index_in_dim(measured, which, 0, False)

        def far_field(wave_in):
            far_wave = transform(far_table, wave_in)
            residual = jnp.sum(far_wave * far_wave, axis=(0, 1)) - target
            return transform(far_adjoint, residual * far_wave).astype(jnp.bfloat16)

        seed_wave = lax.cond(
            my_section == depth_size - 1, far_field, lambda wave_in: zero_wave, out_wave
        )
        seeds = lax.dynamic_update_index_in_dim(seeds, seed_wave, which, 0)
        return (out_wave, saved, seeds)

    def backward_work(which, incoming, saved, seeds, accumulated):
        seed_wave = lax.dynamic_index_in_dim(seeds, which, 0, False)
        grad_in = jnp.where(my_section == depth_size - 1, seed_wave, incoming)
        row_start, col_start = corner(which)
        patch_block = lax.dynamic_slice(extended, (0, row_start, col_start), (2, pixels, pixels))
        grad_lit = transform(prop_adjoint, grad_in)
        in_wave = lax.dynamic_index_in_dim(saved, which, 0, False).astype(jnp.float32)
        grad_term = conj_sum(in_wave, grad_lit)
        current = lax.dynamic_slice(accumulated, (0, row_start, col_start), (2, pixels, pixels))
        accumulated = lax.dynamic_update_slice(
            accumulated, current + grad_term, (0, row_start, col_start)
        )
        out_wave = conj_multiply(patch_block, grad_lit).astype(jnp.bfloat16)
        return (out_wave, accumulated)

    def forward_guarded(which, incoming, saved, seeds):
        active = (which >= 0) & (which < local_count)
        clipped = jnp.clip(which, 0, local_count - 1)
        return lax.cond(
            active,
            lambda operands: forward_work(clipped, operands[0], operands[1], operands[2]),
            lambda operands: (zero_wave, operands[1], operands[2]),
            (incoming, saved, seeds),
        )

    def backward_guarded(which, incoming, saved, seeds, accumulated):
        active = (which >= 0) & (which < local_count)
        clipped = jnp.clip(which, 0, local_count - 1)
        return lax.cond(
            active,
            lambda operands: backward_work(clipped, operands[0], saved, seeds, operands[1]),
            lambda operands: (zero_wave, operands[1]),
            (incoming, accumulated),
        )

    def forward_turn(step_now, carried):
        incoming, saved, seeds = carried
        out_wave, saved, seeds = forward_guarded(step_now - my_section, incoming, saved, seeds)
        incoming = from_behind(out_wave, "depth", 1)
        return (incoming, saved, seeds)

    _, saved, seeds = lax.fori_loop(
        0, local_count + depth_size - 1, forward_turn, (zero_wave, saved_init, saved_init)
    )

    def backward_turn(step_now, carried):
        incoming, accumulated = carried
        which = step_now - (depth_size - 1 - my_section)
        out_wave, accumulated = backward_guarded(which, incoming, saved, seeds, accumulated)
        incoming = from_behind(out_wave, "depth", -1)
        return (incoming, accumulated)

    _, accumulated = lax.fori_loop(
        0, local_count + depth_size - 1, backward_turn, (zero_wave, accum_init)
    )
    carried_over = shifted(accumulated[:, 2 * tile_rows :], "lat", 1)
    middle_rows = accumulated[:, tile_rows : 2 * tile_rows] + carried_over
    total = accumulated[:, :tile_rows] + shifted(middle_rows, "lat", 1)
    return total[None]


def solution(mesh):
    return jax.shard_map(
        on_device,
        mesh=mesh,
        in_specs=(P("depth", None, "lat", None), P(), P("lat", None), P("lat", None, None)),
        out_specs=P("depth", None, "lat", None),
        check_vma=False,
    )
```

profile of v0, /device:TPU:0, one launch (start us, length us, event | category | flops | bytes accessed | tf_op | source)
XLA Modules:
  0.0 799.3 jit_solution(9927761622503507075)
XLA Ops:
  7.4 18.8 %collective-permute-done.2 = f32[2,128,2048]{2,1,0:T(8,128)} collective-permute-done((f32[2,128,2048]{2,1,0:T(8,128)}, f32[2,128,2048]{2,1,0:T(8,128)}, u32[]{:S(2)}, u32[]{:S(2)}) %collective-permute-start.2) | collective-permute-done | bytes 2097184 | tf_op jit(solution)/shard_map/ppermute | solution.py:14
  36.2 15.9 %collective-permute-done.3 = f32[2,128,2048]{2,1,0:T(8,128)} collective-permute-done((f32[2,128,2048]{2,1,0:T(8,128)}, f32[2,128,2048]{2,1,0:T(8,128)}, u32[]{:S(2)}, u32[]{:S(2)}) %collective-permute-start.3) | collective-permute-done | bytes 2097184 | tf_op jit(solution)/shard_map/ppermute | solution.py:14
  61.6 268.0 %while.36 = (s32[]{:T(128)}, bf16[2,2,256,256]{3,2,1,0:T(8,128)(2,1)}, bf16[4,2,2,256,256]{4,3,2,1,0:T(8,128)(2,1)}, bf16[4,2,2,256,256]{4,3,2,1,0:T(8,128)(2,1)...) while((s32[]{:T(128)}, ...), condition=%wide.region_6.7_spmd, body=%wide.region_0.6_spmd.sunk | while | flops 9666822144 | bytes 33293520 | solution.py:156
  61.6 15.0 %conditional.5 = (bf16[2,2,256,256]{3,2,1,0:T(8,128)(2,1)}, bf16[4,2,2,256,256]{4,3,2,1,0:T(8,128)(2,1)}, bf16[4,2,2,256,256]{4,3,2,1,0:T(8,128)(2,1)}) conditional(s32[]{:T(128)} %convert_element_type.183, (bf16[4,2,2,256,256]{4,3,2,1,0:T(8,128)(2,1)}, bf16[4,2,2,256,256]{4,3,2,1,0:T(8,128)(2,1)}) %tuple.116, (s32[]{:T(128)}, s32[4,2]{0,1:T(2,128)S(1)}, ...), branch_computations={%region_1.1_spmd, %region_2.5_spmd} | conditional | flops 9666822144 | bytes 31196036 | solution.py:133
  78.8 11.6 %collective-permute-done = bf16[2,2,256,256]{3,2,1,0:T(8,128)(2,1)} collective-permute-done((bf16[2,2,256,256]{3,2,1,0:T(8,128)(2,1)}, bf16[2,2,256,256]{3,2,1,0:T(8,128)(2,1)}, u32[]{:S(2)}, u32[]{:S(2)}) %collective-permute-start) | collective-permute-done | bytes 524320 | tf_op jit(solution)/shard_map/while/body/eval_jaxpr/ppermute | solution.py:20
  90.4 15.0 %conditional.5 = (bf16[2,2,256,256]{3,2,1,0:T(8,128)(2,1)}, bf16[4,2,2,256,256]{4,3,2,1,0:T(8,128)(2,1)}, bf16[4,2,2,256,256]{4,3,2,1,0:T(8,128)(2,1)}) conditional(s32[]{:T(128)} %convert_element_type.183, (bf16[4,2,2,256,256]{4,3,2,1,0:T(8,128)(2,1)}, bf16[4,2,2,256,256]{4,3,2,1,0:T(8,128)(2,1)}) %tuple.116, (s32[]{:T(128)}, s32[4,2]{0,1:T(2,128)S(1)}, ...), branch_computations={%region_1.1_spmd, %region_2.5_spmd} | conditional | flops 9666822144 | bytes 31196036 | solution.py:133
  110.7 10.9 %collective-permute-done = bf16[2,2,256,256]{3,2,1,0:T(8,128)(2,1)} collective-permute-done((bf16[2,2,256,256]{3,2,1,0:T(8,128)(2,1)}, bf16[2,2,256,256]{3,2,1,0:T(8,128)(2,1)}, u32[]{:S(2)}, u32[]{:S(2)}) %collective-permute-start) | collective-permute-done | bytes 524320 | tf_op jit(solution)/shard_map/while/body/eval_jaxpr/ppermute | solution.py:20
  121.6 15.0 %conditional.5 = (bf16[2,2,256,256]{3,2,1,0:T(8,128)(2,1)}, bf16[4,2,2,256,256]{4,3,2,1,0:T(8,128)(2,1)}, bf16[4,2,2,256,256]{4,3,2,1,0:T(8,128)(2,1)}) conditional(s32[]{:T(128)} %convert_element_type.183, (bf16[4,2,2,256,256]{4,3,2,1,0:T(8,128)(2,1)}, bf16[4,2,2,256,256]{4,3,2,1,0:T(8,128)(2,1)}) %tuple.116, (s32[]{:T(128)}, s32[4,2]{0,1:T(2,128)S(1)}, ...), branch_computations={%region_1.1_spmd, %region_2.5_spmd} | conditional | flops 9666822144 | bytes 31196036 | solution.py:133
  141.8 10.1 %collective-permute-done = bf16[2,2,256,256]{3,2,1,0:T(8,128)(2,1)} collective-permute-done((bf16[2,2,256,256]{3,2,1,0:T(8,128)(2,1)}, bf16[2,2,256,256]{3,2,1,0:T(8,128)(2,1)}, u32[]{:S(2)}, u32[]{:S(2)}) %collective-permute-start) | collective-permute-done | bytes 524320 | tf_op jit(solution)/shard_map/while/body/eval_jaxpr/ppermute | solution.py:20
  151.9 15.0 %conditional.5 = (bf16[2,2,256,256]{3,2,1,0:T(8,128)(2,1)}, bf16[4,2,2,256,256]{4,3,2,1,0:T(8,128)(2,1)}, bf16[4,2,2,256,256]{4,3,2,1,0:T(8,128)(2,1)}) conditional(s32[]{:T(128)} %convert_element_type.183, (bf16[4,2,2,256,256]{4,3,2,1,0:T(8,128)(2,1)}, bf16[4,2,2,256,256]{4,3,2,1,0:T(8,128)(2,1)}) %tuple.116, (s32[]{:T(128)}, s32[4,2]{0,1:T(2,128)S(1)}, ...), branch_computations={%region_1.1_spmd, %region_2.5_spmd} | conditional | flops 9666822144 | bytes 31196036 | solution.py:133
  182.2 19.7 %collective-permute-start = (bf16[2,2,256,256]{3,2,1,0:T(8,128)(2,1)}, bf16[2,2,256,256]{3,2,1,0:T(8,128)(2,1)}, u32[]{:S(2)}, u32[]{:S(2)}) collective-permute-start(bf16[2,2,256,256]{3,2,1,0:T(8,128)(2,1)} %get-tuple-element.789), channel_id=1, source_target_pairs={{0,4},{4,8},{8,12},{12,16},{16,20},{20,24},{24,28},{1,5},{5,9},{9,... | collective-permute-start | bytes 1572872 | tf_op jit(solution)/shard_map/while/body/eval_jaxpr/ppermute | solution.py:20
  225.9 20.3 %collective-permute-start = (bf16[2,2,256,256]{3,2,1,0:T(8,128)(2,1)}, bf16[2,2,256,256]{3,2,1,0:T(8,128)(2,1)}, u32[]{:S(2)}, u32[]{:S(2)}) collective-permute-start(bf16[2,2,256,256]{3,2,1,0:T(8,128)(2,1)} %get-tuple-element.789), channel_id=1, source_target_pairs={{0,4},{4,8},{8,12},{12,16},{16,20},{20,24},{24,28},{1,5},{5,9},{9,... | collective-permute-start | bytes 1572872 | tf_op jit(solution)/shard_map/while/body/eval_jaxpr/ppermute | solution.py:20
  266.9 16.6 %collective-permute-start = (bf16[2,2,256,256]{3,2,1,0:T(8,128)(2,1)}, bf16[2,2,256,256]{3,2,1,0:T(8,128)(2,1)}, u32[]{:S(2)}, u32[]{:S(2)}) collective-permute-start(bf16[2,2,256,256]{3,2,1,0:T(8,128)(2,1)} %get-tuple-element.789), channel_id=1, source_target_pairs={{0,4},{4,8},{8,12},{12,16},{16,20},{20,24},{24,28},{1,5},{5,9},{9,... | collective-permute-start | bytes 1572872 | tf_op jit(solution)/shard_map/while/body/eval_jaxpr/ppermute | solution.py:20
  303.7 19.7 %collective-permute-start = (bf16[2,2,256,256]{3,2,1,0:T(8,128)(2,1)}, bf16[2,2,256,256]{3,2,1,0:T(8,128)(2,1)}, u32[]{:S(2)}, u32[]{:S(2)}) collective-permute-start(bf16[2,2,256,256]{3,2,1,0:T(8,128)(2,1)} %get-tuple-element.789), channel_id=1, source_target_pairs={{0,4},{4,8},{8,12},{12,16},{16,20},{20,24},{24,28},{1,5},{5,9},{9,... | collective-permute-start | bytes 1572872 | tf_op jit(solution)/shard_map/while/body/eval_jaxpr/ppermute | solution.py:20
  333.0 408.4 %while.37 = (s32[]{:T(128)}, bf16[2,2,256,256]{3,2,1,0:T(8,128)(2,1)S(1)}, f32[2,384,2048]{2,1,0:T(8,128)}, s32[]{:T(128)}, s32[4,2]{0,1:T(2,128)S(1)}, /*index=...) while((s32[]{:T(128)}, ...), condition=%wide.region_12.13_spmd, body=%wide.region_7.12_spmd.sunk | while | flops 3224240128 | bytes 18350660 | solution.py:167
  334.4 11.1 %collective-permute-done.1 = bf16[2,2,256,256]{3,2,1,0:T(8,128)(2,1)S(1)} collective-permute-done((bf16[2,2,256,256]{3,2,1,0:T(8,128)(2,1)S(1)}, bf16[2,2,256,256]{3,2,1,0:T(8,128)(2,1)S(1)}, u32[]{:S(2)}, u32[]{:S(2)}) %collective-permute-start.1) | collective-permute-done | bytes 524320 | tf_op jit(solution)/shard_map/while/body/eval_jaxpr/ppermute | solution.py:20
  346.9 20.9 %collective-permute-done.1 = bf16[2,2,256,256]{3,2,1,0:T(8,128)(2,1)S(1)} collective-permute-done((bf16[2,2,256,256]{3,2,1,0:T(8,128)(2,1)S(1)}, bf16[2,2,256,256]{3,2,1,0:T(8,128)(2,1)S(1)}, u32[]{:S(2)}, u32[]{:S(2)}) %collective-permute-start.1) | collective-permute-done | bytes 524320 | tf_op jit(solution)/shard_map/while/body/eval_jaxpr/ppermute | solution.py:20
  369.1 14.6 %collective-permute-done.1 = bf16[2,2,256,256]{3,2,1,0:T(8,128)(2,1)S(1)} collective-permute-done((bf16[2,2,256,256]{3,2,1,0:T(8,128)(2,1)S(1)}, bf16[2,2,256,256]{3,2,1,0:T(8,128)(2,1)S(1)}, u32[]{:S(2)}, u32[]{:S(2)}) %collective-permute-start.1) | collective-permute-done | bytes 524320 | tf_op jit(solution)/shard_map/while/body/eval_jaxpr/ppermute | solution.py:20
  385.1 33.1 %collective-permute-done.1 = bf16[2,2,256,256]{3,2,1,0:T(8,128)(2,1)S(1)} collective-permute-done((bf16[2,2,256,256]{3,2,1,0:T(8,128)(2,1)S(1)}, bf16[2,2,256,256]{3,2,1,0:T(8,128)(2,1)S(1)}, u32[]{:S(2)}, u32[]{:S(2)}) %collective-permute-start.1) | collective-permute-done | bytes 524320 | tf_op jit(solution)/shard_map/while/body/eval_jaxpr/ppermute | solution.py:20
  419.5 18.9 %collective-permute-done.1 = bf16[2,2,256,256]{3,2,1,0:T(8,128)(2,1)S(1)} collective-permute-done((bf16[2,2,256,256]{3,2,1,0:T(8,128)(2,1)S(1)}, bf16[2,2,256,256]{3,2,1,0:T(8,128)(2,1)S(1)}, u32[]{:S(2)}, u32[]{:S(2)}) %collective-permute-start.1) | collective-permute-done | bytes 524320 | tf_op jit(solution)/shard_map/while/body/eval_jaxpr/ppermute | solution.py:20
  439.8 33.1 %collective-permute-done.1 = bf16[2,2,256,256]{3,2,1,0:T(8,128)(2,1)S(1)} collective-permute-done((bf16[2,2,256,256]{3,2,1,0:T(8,128)(2,1)S(1)}, bf16[2,2,256,256]{3,2,1,0:T(8,128)(2,1)S(1)}, u32[]{:S(2)}, u32[]{:S(2)}) %collective-permute-start.1) | collective-permute-done | bytes 524320 | tf_op jit(solution)/shard_map/while/body/eval_jaxpr/ppermute | solution.py:20
  474.3 139.7 %collective-permute-done.1 = bf16[2,2,256,256]{3,2,1,0:T(8,128)(2,1)S(1)} collective-permute-done((bf16[2,2,256,256]{3,2,1,0:T(8,128)(2,1)S(1)}, bf16[2,2,256,256]{3,2,1,0:T(8,128)(2,1)S(1)}, u32[]{:S(2)}, u32[]{:S(2)}) %collective-permute-start.1) | collective-permute-done | bytes 524320 | tf_op jit(solution)/shard_map/while/body/eval_jaxpr/ppermute | solution.py:20
  613.9 18.6 %conditional.6 = (bf16[2,2,256,256]{3,2,1,0:T(8,128)(2,1)S(1)}, f32[2,384,2048]{2,1,0:T(8,128)}) conditional(s32[]{:T(128)} %convert_element_type.184, f32[2,384,2048]{2,1,0:T(8,128)} %get-tuple-element.874, (s32[]{:T(128)}, s32[4,2]{0,1:T(2,128)S(1)}, f32[2,384,2048]{2,1,0:T(8,128)}, s32[]{:T(128)}, bf16[4,2,2,256,256]{4,3,2,1,0:T(8,128)(2,1)}, ...), branch_computations={%region_8.8_spmd, %region_9.11_spmd} | conditional | flops 3224240128 | bytes 16253235 | solution.py:143
  633.9 14.2 %collective-permute-done.1 = bf16[2,2,256,256]{3,2,1,0:T(8,128)(2,1)S(1)} collective-permute-done((bf16[2,2,256,256]{3,2,1,0:T(8,128)(2,1)S(1)}, bf16[2,2,256,256]{3,2,1,0:T(8,128)(2,1)S(1)}, u32[]{:S(2)}, u32[]{:S(2)}) %collective-permute-start.1) | collective-permute-done | bytes 524320 | tf_op jit(solution)/shard_map/while/body/eval_jaxpr/ppermute | solution.py:20
  648.1 19.4 %conditional.6 = (bf16[2,2,256,256]{3,2,1,0:T(8,128)(2,1)S(1)}, f32[2,384,2048]{2,1,0:T(8,128)}) conditional(s32[]{:T(128)} %convert_element_type.184, f32[2,384,2048]{2,1,0:T(8,128)} %get-tuple-element.874, (s32[]{:T(128)}, s32[4,2]{0,1:T(2,128)S(1)}, f32[2,384,2048]{2,1,0:T(8,128)}, s32[]{:T(128)}, bf16[4,2,2,256,256]{4,3,2,1,0:T(8,128)(2,1)}, ...), branch_computations={%region_8.8_spmd, %region_9.11_spmd} | conditional | flops 3224240128 | bytes 16253235 | solution.py:143
  668.7 10.6 %collective-permute-done.1 = bf16[2,2,256,256]{3,2,1,0:T(8,128)(2,1)S(1)} collective-permute-done((bf16[2,2,256,256]{3,2,1,0:T(8,128)(2,1)S(1)}, bf16[2,2,256,256]{3,2,1,0:T(8,128)(2,1)S(1)}, u32[]{:S(2)}, u32[]{:S(2)}) %collective-permute-start.1) | collective-permute-done | bytes 524320 | tf_op jit(solution)/shard_map/while/body/eval_jaxpr/ppermute | solution.py:20
  679.3 19.3 %conditional.6 = (bf16[2,2,256,256]{3,2,1,0:T(8,128)(2,1)S(1)}, f32[2,384,2048]{2,1,0:T(8,128)}) conditional(s32[]{:T(128)} %convert_element_type.184, f32[2,384,2048]{2,1,0:T(8,128)} %get-tuple-element.874, (s32[]{:T(128)}, s32[4,2]{0,1:T(2,128)S(1)}, f32[2,384,2048]{2,1,0:T(8,128)}, s32[]{:T(128)}, bf16[4,2,2,256,256]{4,3,2,1,0:T(8,128)(2,1)}, ...), branch_computations={%region_8.8_spmd, %region_9.11_spmd} | conditional | flops 3224240128 | bytes 16253235 | solution.py:143
  699.9 11.0 %collective-permute-done.1 = bf16[2,2,256,256]{3,2,1,0:T(8,128)(2,1)S(1)} collective-permute-done((bf16[2,2,256,256]{3,2,1,0:T(8,128)(2,1)S(1)}, bf16[2,2,256,256]{3,2,1,0:T(8,128)(2,1)S(1)}, u32[]{:S(2)}, u32[]{:S(2)}) %collective-permute-start.1) | collective-permute-done | bytes 524320 | tf_op jit(solution)/shard_map/while/body/eval_jaxpr/ppermute | solution.py:20
  710.9 19.4 %conditional.6 = (bf16[2,2,256,256]{3,2,1,0:T(8,128)(2,1)S(1)}, f32[2,384,2048]{2,1,0:T(8,128)}) conditional(s32[]{:T(128)} %convert_element_type.184, f32[2,384,2048]{2,1,0:T(8,128)} %get-tuple-element.874, (s32[]{:T(128)}, s32[4,2]{0,1:T(2,128)S(1)}, f32[2,384,2048]{2,1,0:T(8,128)}, s32[]{:T(128)}, bf16[4,2,2,256,256]{4,3,2,1,0:T(8,128)(2,1)}, ...), branch_computations={%region_8.8_spmd, %region_9.11_spmd} | conditional | flops 3224240128 | bytes 16253235 | solution.py:143
  731.6 9.8 %collective-permute-done.1 = bf16[2,2,256,256]{3,2,1,0:T(8,128)(2,1)S(1)} collective-permute-done((bf16[2,2,256,256]{3,2,1,0:T(8,128)(2,1)S(1)}, bf16[2,2,256,256]{3,2,1,0:T(8,128)(2,1)S(1)}, u32[]{:S(2)}, u32[]{:S(2)}) %collective-permute-start.1) | collective-permute-done | bytes 524320 | tf_op jit(solution)/shard_map/while/body/eval_jaxpr/ppermute | solution.py:20
  743.2 25.4 %collective-permute-done.4 = f32[2,128,2048]{2,1,0:T(8,128)S(1)} collective-permute-done((f32[2,128,2048]{2,1,0:T(8,128)S(1)}, f32[2,128,2048]{2,1,0:T(8,128)S(1)}, u32[]{:S(2)}, u32[]{:S(2)}) %collective-permute-start.4) | collective-permute-done | bytes 2097184 | tf_op jit(solution)/shard_map/ppermute | solution.py:14
  772.7 23.3 %collective-permute-done.5 = f32[2,128,2048]{2,1,0:T(8,128)S(1)} collective-permute-done((f32[2,128,2048]{2,1,0:T(8,128)S(1)}, f32[2,128,2048]{2,1,0:T(8,128)S(1)}, u32[]{:S(2)}, u32[]{:S(2)}) %collective-permute-start.5) | collective-permute-done | bytes 2097184 | tf_op jit(solution)/shard_map/ppermute | solution.py:14
  (169 shorter events, 266.2 us)
Async XLA Ops:
  0.0 26.2 %collective-permute-start.2 = (f32[2,128,2048]{2,1,0:T(8,128)}, f32[2,128,2048]{2,1,0:T(8,128)}, u32[]{:S(2)}, u32[]{:S(2)}) collective-permute-start(f32[2,128,2048]{2,1,0:T(8,128)} %bitcast.176), channel_id=1, source_target_pairs={{1,0},{2,1},{3,2},{0,3},{5,4},{6,5},{7,6},{4,7},{9,8},{10,9},{11,1... | collective-permute-start | bytes 6291464 | tf_op jit(solution)/shard_map/ppermute | solution.py:14
  26.2 25.8 %collective-permute-start.3 = (f32[2,128,2048]{2,1,0:T(8,128)}, f32[2,128,2048]{2,1,0:T(8,128)}, u32[]{:S(2)}, u32[]{:S(2)}) collective-permute-start(f32[2,128,2048]{2,1,0:T(8,128)} %collective-permute-done.2), channel_id=1, source_target_pairs={{1,0},{2,1},{3,2},{0,3},{5,4},{6,5},{7,6},{4,7},{9,8},{10,9},{11,1... | collective-permute-start | bytes 6291464 | tf_op jit(solution)/shard_map/ppermute | solution.py:14
  35.0 17.1 %copy-start.1 = (f32[1,2,128,2048]{3,2,1,0:T(8,128)S(1)}, f32[1,2,128,2048]{3,2,1,0:T(8,128)}, u32[]{:S(2)}) copy-start(f32[1,2,128,2048]{3,2,1,0:T(8,128)} %param.14) | copy-start | bytes 6291460
  58.5 3.1 copy-start.2
  76.6 13.7 %collective-permute-start = (bf16[2,2,256,256]{3,2,1,0:T(8,128)(2,1)}, bf16[2,2,256,256]{3,2,1,0:T(8,128)(2,1)}, u32[]{:S(2)}, u32[]{:S(2)}) collective-permute-start(bf16[2,2,256,256]{3,2,1,0:T(8,128)(2,1)} %get-tuple-element.789), channel_id=1, source_target_pairs={{0,4},{4,8},{8,12},{12,16},{16,20},{20,24},{24,28},{1,5},{5,9},{9,... | collective-permute-start | bytes 1572872 | tf_op jit(solution)/shard_map/while/body/eval_jaxpr/ppermute | solution.py:20
  105.4 16.2 %collective-permute-start = (bf16[2,2,256,256]{3,2,1,0:T(8,128)(2,1)}, bf16[2,2,256,256]{3,2,1,0:T(8,128)(2,1)}, u32[]{:S(2)}, u32[]{:S(2)}) collective-permute-start(bf16[2,2,256,256]{3,2,1,0:T(8,128)(2,1)} %get-tuple-element.789), channel_id=1, source_target_pairs={{0,4},{4,8},{8,12},{12,16},{16,20},{20,24},{24,28},{1,5},{5,9},{9,... | collective-permute-start | bytes 1572872 | tf_op jit(solution)/shard_map/while/body/eval_jaxpr/ppermute | solution.py:20
  136.6 15.3 %collective-permute-start = (bf16[2,2,256,256]{3,2,1,0:T(8,128)(2,1)}, bf16[2,2,256,256]{3,2,1,0:T(8,128)(2,1)}, u32[]{:S(2)}, u32[]{:S(2)}) collective-permute-start(bf16[2,2,256,256]{3,2,1,0:T(8,128)(2,1)} %get-tuple-element.789), channel_id=1, source_target_pairs={{0,4},{4,8},{8,12},{12,16},{16,20},{20,24},{24,28},{1,5},{5,9},{9,... | collective-permute-start | bytes 1572872 | tf_op jit(solution)/shard_map/while/body/eval_jaxpr/ppermute | solution.py:20
  167.0 14.4 %collective-permute-start = (bf16[2,2,256,256]{3,2,1,0:T(8,128)(2,1)}, bf16[2,2,256,256]{3,2,1,0:T(8,128)(2,1)}, u32[]{:S(2)}, u32[]{:S(2)}) collective-permute-start(bf16[2,2,256,256]{3,2,1,0:T(8,128)(2,1)} %get-tuple-element.789), channel_id=1, source_target_pairs={{0,4},{4,8},{8,12},{12,16},{16,20},{20,24},{24,28},{1,5},{5,9},{9,... | collective-permute-start | bytes 1572872 | tf_op jit(solution)/shard_map/while/body/eval_jaxpr/ppermute | solution.py:20
  182.2 28.3 %collective-permute-start = (bf16[2,2,256,256]{3,2,1,0:T(8,128)(2,1)}, bf16[2,2,256,256]{3,2,1,0:T(8,128)(2,1)}, u32[]{:S(2)}, u32[]{:S(2)}) collective-permute-start(bf16[2,2,256,256]{3,2,1,0:T(8,128)(2,1)} %get-tuple-element.789), channel_id=1, source_target_pairs={{0,4},{4,8},{8,12},{12,16},{16,20},{20,24},{24,28},{1,5},{5,9},{9,... | collective-permute-start | bytes 1572872 | tf_op jit(solution)/shard_map/while/body/eval_jaxpr/ppermute | solution.py:20
  211.3 13.8 %collective-permute-start = (bf16[2,2,256,256]{3,2,1,0:T(8,128)(2,1)}, bf16[2,2,256,256]{3,2,1,0:T(8,128)(2,1)}, u32[]{:S(2)}, u32[]{:S(2)}) collective-permute-start(bf16[2,2,256,256]{3,2,1,0:T(8,128)(2,1)} %get-tuple-element.789), channel_id=1, source_target_pairs={{0,4},{4,8},{8,12},{12,16},{16,20},{20,24},{24,28},{1,5},{5,9},{9,... | collective-permute-start | bytes 1572872 | tf_op jit(solution)/shard_map/while/body/eval_jaxpr/ppermute | solution.py:20
  225.9 27.1 %collective-permute-start = (bf16[2,2,256,256]{3,2,1,0:T(8,128)(2,1)}, bf16[2,2,256,256]{3,2,1,0:T(8,128)(2,1)}, u32[]{:S(2)}, u32[]{:S(2)}) collective-permute-start(bf16[2,2,256,256]{3,2,1,0:T(8,128)(2,1)} %get-tuple-element.789), channel_id=1, source_target_pairs={{0,4},{4,8},{8,12},{12,16},{16,20},{20,24},{24,28},{1,5},{5,9},{9,... | collective-permute-start | bytes 1572872 | tf_op jit(solution)/shard_map/while/body/eval_jaxpr/ppermute | solution.py:20
  253.8 12.3 %collective-permute-start = (bf16[2,2,256,256]{3,2,1,0:T(8,128)(2,1)}, bf16[2,2,256,256]{3,2,1,0:T(8,128)(2,1)}, u32[]{:S(2)}, u32[]{:S(2)}) collective-permute-start(bf16[2,2,256,256]{3,2,1,0:T(8,128)(2,1)} %get-tuple-element.789), channel_id=1, source_target_pairs={{0,4},{4,8},{8,12},{12,16},{16,20},{20,24},{24,28},{1,5},{5,9},{9,... | collective-permute-start | bytes 1572872 | tf_op jit(solution)/shard_map/while/body/eval_jaxpr/ppermute | solution.py:20
  266.9 22.9 %collective-permute-start = (bf16[2,2,256,256]{3,2,1,0:T(8,128)(2,1)}, bf16[2,2,256,256]{3,2,1,0:T(8,128)(2,1)}, u32[]{:S(2)}, u32[]{:S(2)}) collective-permute-start(bf16[2,2,256,256]{3,2,1,0:T(8,128)(2,1)} %get-tuple-element.789), channel_id=1, source_target_pairs={{0,4},{4,8},{8,12},{12,16},{16,20},{20,24},{24,28},{1,5},{5,9},{9,... | collective-permute-start | bytes 1572872 | tf_op jit(solution)/shard_map/while/body/eval_jaxpr/ppermute | solution.py:20
  290.7 12.1 %collective-permute-start = (bf16[2,2,256,256]{3,2,1,0:T(8,128)(2,1)}, bf16[2,2,256,256]{3,2,1,0:T(8,128)(2,1)}, u32[]{:S(2)}, u32[]{:S(2)}) collective-permute-start(bf16[2,2,256,256]{3,2,1,0:T(8,128)(2,1)} %get-tuple-element.789), channel_id=1, source_target_pairs={{0,4},{4,8},{8,12},{12,16},{16,20},{20,24},{24,28},{1,5},{5,9},{9,... | collective-permute-start | bytes 1572872 | tf_op jit(solution)/shard_map/while/body/eval_jaxpr/ppermute | solution.py:20
  303.7 25.9 %collective-permute-start = (bf16[2,2,256,256]{3,2,1,0:T(8,128)(2,1)}, bf16[2,2,256,256]{3,2,1,0:T(8,128)(2,1)}, u32[]{:S(2)}, u32[]{:S(2)}) collective-permute-start(bf16[2,2,256,256]{3,2,1,0:T(8,128)(2,1)} %get-tuple-element.789), channel_id=1, source_target_pairs={{0,4},{4,8},{8,12},{12,16},{16,20},{20,24},{24,28},{1,5},{5,9},{9,... | collective-permute-start | bytes 1572872 | tf_op jit(solution)/shard_map/while/body/eval_jaxpr/ppermute | solution.py:20
  333.0 12.4 %collective-permute-start.1 = (bf16[2,2,256,256]{3,2,1,0:T(8,128)(2,1)S(1)}, bf16[2,2,256,256]{3,2,1,0:T(8,128)(2,1)S(1)}, u32[]{:S(2)}, u32[]{:S(2)}) collective-permute-start(bf16[2,2,256,256]{3,2,1,0:T(8,128)(2,1)S(1)} %get-tuple-element.802), channel_id=1, source_target_pairs={{4,0},{8,4},{12,8},{16,12},{20,16},{24,20},{28,24},{5,1},{9,5},{13... | collective-permute-start | bytes 1572872 | tf_op jit(solution)/shard_map/while/body/eval_jaxpr/ppermute | solution.py:20
  345.5 22.2 %collective-permute-start.1 = (bf16[2,2,256,256]{3,2,1,0:T(8,128)(2,1)S(1)}, bf16[2,2,256,256]{3,2,1,0:T(8,128)(2,1)S(1)}, u32[]{:S(2)}, u32[]{:S(2)}) collective-permute-start(bf16[2,2,256,256]{3,2,1,0:T(8,128)(2,1)S(1)} %get-tuple-element.802), channel_id=1, source_target_pairs={{4,0},{8,4},{12,8},{16,12},{20,16},{24,20},{28,24},{5,1},{9,5},{13... | collective-permute-start | bytes 1572872 | tf_op jit(solution)/shard_map/while/body/eval_jaxpr/ppermute | solution.py:20
  367.8 15.9 %collective-permute-start.1 = (bf16[2,2,256,256]{3,2,1,0:T(8,128)(2,1)S(1)}, bf16[2,2,256,256]{3,2,1,0:T(8,128)(2,1)S(1)}, u32[]{:S(2)}, u32[]{:S(2)}) collective-permute-start(bf16[2,2,256,256]{3,2,1,0:T(8,128)(2,1)S(1)} %get-tuple-element.802), channel_id=1, source_target_pairs={{4,0},{8,4},{12,8},{16,12},{20,16},{24,20},{28,24},{5,1},{9,5},{13... | collective-permute-start | bytes 1572872 | tf_op jit(solution)/shard_map/while/body/eval_jaxpr/ppermute | solution.py:20
  383.8 34.4 %collective-permute-start.1 = (bf16[2,2,256,256]{3,2,1,0:T(8,128)(2,1)S(1)}, bf16[2,2,256,256]{3,2,1,0:T(8,128)(2,1)S(1)}, u32[]{:S(2)}, u32[]{:S(2)}) collective-permute-start(bf16[2,2,256,256]{3,2,1,0:T(8,128)(2,1)S(1)} %get-tuple-element.802), channel_id=1, source_target_pairs={{4,0},{8,4},{12,8},{16,12},{20,16},{24,20},{28,24},{5,1},{9,5},{13... | collective-permute-start | bytes 1572872 | tf_op jit(solution)/shard_map/while/body/eval_jaxpr/ppermute | solution.py:20
  418.2 20.2 %collective-permute-start.1 = (bf16[2,2,256,256]{3,2,1,0:T(8,128)(2,1)S(1)}, bf16[2,2,256,256]{3,2,1,0:T(8,128)(2,1)S(1)}, u32[]{:S(2)}, u32[]{:S(2)}) collective-permute-start(bf16[2,2,256,256]{3,2,1,0:T(8,128)(2,1)S(1)} %get-tuple-element.802), channel_id=1, source_target_pairs={{4,0},{8,4},{12,8},{16,12},{20,16},{24,20},{28,24},{5,1},{9,5},{13... | collective-permute-start | bytes 1572872 | tf_op jit(solution)/shard_map/while/body/eval_jaxpr/ppermute | solution.py:20
  438.5 34.4 %collective-permute-start.1 = (bf16[2,2,256,256]{3,2,1,0:T(8,128)(2,1)S(1)}, bf16[2,2,256,256]{3,2,1,0:T(8,128)(2,1)S(1)}, u32[]{:S(2)}, u32[]{:S(2)}) collective-permute-start(bf16[2,2,256,256]{3,2,1,0:T(8,128)(2,1)S(1)} %get-tuple-element.802), channel_id=1, source_target_pairs={{4,0},{8,4},{12,8},{16,12},{20,16},{24,20},{28,24},{5,1},{9,5},{13... | collective-permute-start | bytes 1572872 | tf_op jit(solution)/shard_map/while/body/eval_jaxpr/ppermute | solution.py:20
  473.0 141.0 %collective-permute-start.1 = (bf16[2,2,256,256]{3,2,1,0:T(8,128)(2,1)S(1)}, bf16[2,2,256,256]{3,2,1,0:T(8,128)(2,1)S(1)}, u32[]{:S(2)}, u32[]{:S(2)}) collective-permute-start(bf16[2,2,256,256]{3,2,1,0:T(8,128)(2,1)S(1)} %get-tuple-element.802), channel_id=1, source_target_pairs={{4,0},{8,4},{12,8},{16,12},{20,16},{24,20},{28,24},{5,1},{9,5},{13... | collective-permute-start | bytes 1572872 | tf_op jit(solution)/shard_map/while/body/eval_jaxpr/ppermute | solution.py:20
  632.6 15.5 %collective-permute-start.1 = (bf16[2,2,256,256]{3,2,1,0:T(8,128)(2,1)S(1)}, bf16[2,2,256,256]{3,2,1,0:T(8,128)(2,1)S(1)}, u32[]{:S(2)}, u32[]{:S(2)}) collective-permute-start(bf16[2,2,256,256]{3,2,1,0:T(8,128)(2,1)S(1)} %get-tuple-element.802), channel_id=1, source_target_pairs={{4,0},{8,4},{12,8},{16,12},{20,16},{24,20},{28,24},{5,1},{9,5},{13... | collective-permute-start | bytes 1572872 | tf_op jit(solution)/shard_map/while/body/eval_jaxpr/ppermute | solution.py:20
  667.4 11.9 %collective-permute-start.1 = (bf16[2,2,256,256]{3,2,1,0:T(8,128)(2,1)S(1)}, bf16[2,2,256,256]{3,2,1,0:T(8,128)(2,1)S(1)}, u32[]{:S(2)}, u32[]{:S(2)}) collective-permute-start(bf16[2,2,256,256]{3,2,1,0:T(8,128)(2,1)S(1)} %get-tuple-element.802), channel_id=1, source_target_pairs={{4,0},{8,4},{12,8},{16,12},{20,16},{24,20},{28,24},{5,1},{9,5},{13... | collective-permute-start | bytes 1572872 | tf_op jit(solution)/shard_map/while/body/eval_jaxpr/ppermute | solution.py:20
  698.7 12.3 %collective-permute-start.1 = (bf16[2,2,256,256]{3,2,1,0:T(8,128)(2,1)S(1)}, bf16[2,2,256,256]{3,2,1,0:T(8,128)(2,1)S(1)}, u32[]{:S(2)}, u32[]{:S(2)}) collective-permute-start(bf16[2,2,256,256]{3,2,1,0:T(8,128)(2,1)S(1)} %get-tuple-element.802), channel_id=1, source_target_pairs={{4,0},{8,4},{12,8},{16,12},{20,16},{24,20},{28,24},{5,1},{9,5},{13... | collective-permute-start | bytes 1572872 | tf_op jit(solution)/shard_map/while/body/eval_jaxpr/ppermute | solution.py:20
  730.3 11.1 %collective-permute-start.1 = (bf16[2,2,256,256]{3,2,1,0:T(8,128)(2,1)S(1)}, bf16[2,2,256,256]{3,2,1,0:T(8,128)(2,1)S(1)}, u32[]{:S(2)}, u32[]{:S(2)}) collective-permute-start(bf16[2,2,256,256]{3,2,1,0:T(8,128)(2,1)S(1)} %get-tuple-element.802), channel_id=1, source_target_pairs={{4,0},{8,4},{12,8},{16,12},{20,16},{24,20},{28,24},{5,1},{9,5},{13... | collective-permute-start | bytes 1572872 | tf_op jit(solution)/shard_map/while/body/eval_jaxpr/ppermute | solution.py:20
  743.1 25.5 %collective-permute-start.4 = (f32[2,128,2048]{2,1,0:T(8,128)S(1)}, f32[2,128,2048]{2,1,0:T(8,128)S(1)}, u32[]{:S(2)}, u32[]{:S(2)}) collective-permute-start(f32[2,128,2048]{2,1,0:T(8,128)S(1)} %slice.85), channel_id=1, source_target_pairs={{3,0},{0,1},{1,2},{2,3},{7,4},{4,5},{5,6},{6,7},{11,8},{8,9},{9,10... | collective-permute-start | bytes 6291464 | tf_op jit(solution)/shard_map/ppermute | solution.py:14
  770.5 25.5 %collective-permute-start.5 = (f32[2,128,2048]{2,1,0:T(8,128)S(1)}, f32[2,128,2048]{2,1,0:T(8,128)S(1)}, u32[]{:S(2)}, u32[]{:S(2)}) collective-permute-start(f32[2,128,2048]{2,1,0:T(8,128)S(1)} %slice_add_fusion), channel_id=1, source_target_pairs={{3,0},{0,1},{1,2},{2,3},{7,4},{4,5},{5,6},{6,7},{11,8},{8,9},{9,10... | collective-permute-start | bytes 6291464 | tf_op jit(solution)/shard_map/ppermute | solution.py:14
where the time goes:
time: 804 us; the launch traced here: 799 us
  waiting for transfers between devices  490 us (61%)
  starting transfers between devices  133 us (17%)
  local copies, waits for them, and re-layouts  60.3 us (8%)
  other arithmetic  43.2 us (5%)
  matrix products  39.7 us (5%)
  loops' own time  32.9 us (4%)
    ppermute x22, waiting for transfers between devices, from_behind(): return lax.ppermute(block, axis, route)  407 us
    ppermute x22, starting transfers between devices, from_behind(): return lax.ppermute(block, axis, route)  126 us
    ppermute x4, waiting for transfers between devices, shifted(): return lax.ppermute(block, axis, route)  83.4 us
    dynamic_update_slice x4, local copies, waits for them, and re-layouts, backward_work(): lax.dynamic_update_slice(accumulated, current + grad_term, (0, row_start,...  25.4 us
    dot_general x8, matrix products, transform(): return jnp.einsum('mrik,srlk->msil', middle, table, precision=highest)  18.1 us
    another operation x11, loops' own time, forward_guarded(): lax.cond(active, lambda operands: forward_work(clipped, operands[0], oper...  16.5 us
    another operation x11, loops' own time, backward_guarded(): lax.cond(active, lambda operands: backward_work(clipped, operands[0], sav...  16.2 us
  transfers between devices with their start and end apart: 26, of which 26 were waited for; matrix products, arithmetic and copies ran while one was open for 2% of the time, Pallas kernels for 0%

commit v1 on v0

v1 whole, which is shorter than its diff:
```python
import functools
import math

import jax
import jax.numpy as jnp
import ml_dtypes
import numpy as np
from jax import lax
from jax.experimental import pallas as pl
from jax.experimental.pallas import tpu as pltpu
from jax.sharding import PartitionSpec as P

fresnel = 0.5
MESH = pl.DeviceIdType.MESH
TILES = 3
LANES = 128
VMEM_BYTES = 48 * 1024 * 1024


def shifted(block, axis, distance):
    devices = range(lax.axis_size(axis))
    route = [((i - distance) % len(devices), i) for i in devices]
    return lax.ppermute(block, axis, route)


def host_tables(pixels):
    idx = np.arange(pixels)
    angle = 2.0 * np.pi * (np.outer(idx, idx) % pixels) / pixels
    far = np.exp(-1j * angle) / math.sqrt(pixels)
    freq = np.where(idx < pixels // 2, idx, idx - pixels).astype(np.float64)
    prop = (np.conj(far) * np.exp(-1j * np.pi * fresnel * freq * freq / pixels)[None, :]) @ far

    def block(table):
        return np.block([[table.real, -table.imag], [table.imag, table.real]])

    prop_block, far_block = block(prop), block(far)
    tables = np.stack([prop_block, prop_block.T, far_block, far_block.T])
    high = tables.astype(ml_dtypes.bfloat16)
    rest = (tables - high.astype(np.float64)).astype(ml_dtypes.bfloat16)
    return jnp.asarray(np.stack([high, rest], axis=1))


def window_place(positions_ref, j, k, tile_rows, col_tiles):
    row = lax.rem(positions_ref[j, k, 0], tile_rows)
    col = positions_ref[j, k, 1]
    first = jnp.minimum(col // LANES, col_tiles - 3)
    return row, first, col - first * LANES


def extract_kernel(positions_ref, tile_ref, blocks_ref):
    _, tile_rows, cols = tile_ref.shape
    _, count, _, _, pixels = blocks_ref.shape
    wide = pixels + LANES

    for j in range(TILES):

        @pl.loop(0, count)
        def _(k):
            row, first, shift = window_place(positions_ref, j, k, tile_rows, cols // LANES)
            start = pl.multiple_of(first * LANES, LANES)
            for part in range(2):
                piece = tile_ref[part, :, pl.ds(start, wide)]
                piece = pltpu.roll(piece, lax.rem(wide - shift, wide), 1)[:, :pixels]
                piece = pltpu.roll(piece, lax.rem(tile_rows - row, tile_rows), 0)
                blocks_ref[j, k, part] = piece.astype(blocks_ref.dtype)


def gather_kernel(positions_ref, terms_ref, grad_ref):
    _, tile_rows, cols = grad_ref.shape
    _, count, _, _, pixels = terms_ref.shape
    wide = pixels + LANES
    grad_ref[...] = jnp.zeros_like(grad_ref)

    for j in range(TILES):

        @pl.loop(0, count)
        def _(k):
            row, first, shift = window_place(positions_ref, j, k, tile_rows, cols // LANES)
            start = pl.multiple_of(first * LANES, LANES)
            for part in range(2):
                piece = terms_ref[j, k, part].astype(jnp.float32)
                piece = pltpu.roll(piece, row, 0)
                piece = jnp.concatenate(
                    [piece, jnp.zeros((tile_rows, LANES), jnp.float32)], axis=1
                )
                piece = pltpu.roll(piece, shift, 1)
                grad_ref[part, :, pl.ds(start, wide)] += piece


def spread(count, sections, lats):
    stride = sections // count
    me = lax.axis_index("depth")
    lat = lax.axis_index("lat")
    works = (lax.rem(me, stride) == lax.rem(lat, stride)) & (me // stride < count)
    return stride, me, lat, works


def worker_of(j, k, lat, lats, stride):
    owner = lax.rem(lat - j + lats, lats)
    return {"depth": k * stride + lax.rem(owner, stride), "lat": owner}


def scatter_kernel(
    count, sections, lats, blocks_ref, held_ref, send_sem, recv_sem, own_sem
):
    stride, me, lat, works = spread(count, sections, lats)
    barrier = pltpu.get_barrier_semaphore()

    @pl.when(works)
    def _():
        for j in range(TILES):
            for s in range(sections):

                @pl.when((s != me) if j == 0 else True)
                def _():
                    pl.semaphore_signal(
                        barrier,
                        inc=1,
                        device_id={"depth": s, "lat": lax.rem(lat + j, lats)},
                        device_id_type=MESH,
                    )

    pl.semaphore_wait(barrier, TILES * count - works.astype(jnp.int32))

    def outgoing(j, k):
        return pltpu.make_async_remote_copy(
            src_ref=blocks_ref.at[j, k],
            dst_ref=held_ref.at[me, j],
            send_sem=send_sem.at[j, k],
            recv_sem=recv_sem.at[me, j],
            device_id=worker_of(j, k, lat, lats, stride),
            device_id_type=MESH,
        )

    def own(k):
        return pltpu.make_async_copy(blocks_ref.at[0, k], held_ref.at[me, 0], own_sem)

    def each(remote, local):
        for j in range(TILES):
            for k in range(count):
                if j == 0:
                    mine = works & (me // stride == k)
                    pl.when(mine)(functools.partial(local, k))
                    pl.when(jnp.logical_not(mine))(functools.partial(remote, j, k))
                else:
                    remote(j, k)

    each(lambda j, k: outgoing(j, k).start(), lambda k: own(k).start())
    each(lambda j, k: outgoing(j, k).wait_send(), lambda k: own(k).wait())

    @pl.when(works)
    def _():
        for j in range(TILES):
            for s in range(sections):

                @pl.when((s != me) if j == 0 else True)
                def _():
                    pltpu.make_async_remote_copy(
                        src_ref=blocks_ref.at[0, 0],
                        dst_ref=held_ref.at[s, j],
                        send_sem=send_sem.at[0, 0],
                        recv_sem=recv_sem.at[s, j],
                        device_id={"depth": s, "lat": lax.rem(lat + j, lats)},
                        device_id_type=MESH,
                    ).wait_recv()


def return_kernel(
    count, sections, lats, made_ref, terms_ref, send_sem, recv_sem, own_sem
):
    stride, me, lat, works = spread(count, sections, lats)
    barrier = pltpu.get_barrier_semaphore()
    my_window = me // stride

    def each(remote, local):
        for j in range(TILES):
            for k in range(count):
                if j == 0:
                    mine = works & (my_window == k)
                    if local is not None:
                        pl.when(mine)(functools.partial(local, k))
                    pl.when(jnp.logical_not(mine))(functools.partial(remote, j, k))
                else:
                    remote(j, k)

    each(
        lambda j, k: pl.semaphore_signal(
            barrier,
            inc=1,
            device_id=worker_of(j, k, lat, lats, stride),
            device_id_type=MESH,
        ),
        None,
    )

    def outgoing(s, j):
        return pltpu.make_async_remote_copy(
            src_ref=made_ref.at[s, j],
            dst_ref=terms_ref.at[j, my_window],
            send_sem=send_sem.at[s, j],
            recv_sem=recv_sem.at[j, my_window],
            device_id={"depth": s, "lat": lax.rem(lat + j, lats)},
            device_id_type=MESH,
        )

    def own():
        return pltpu.make_async_copy(
            made_ref.at[me, 0], terms_ref.at[0, my_window], own_sem
        )

    @pl.when(works)
    def _():
        pl.semaphore_wait(barrier, TILES * sections - 1)
        own().start()
        for wait in (False, True):
            for s in range(sections):
                for j in range(TILES):

                    @pl.when((s != me) if j == 0 else True)
                    def _():
                        copy = outgoing(s, j)
                        copy.wait_send() if wait else copy.start()

        own().wait()

    each(
        lambda j, k: pltpu.make_async_remote_copy(
            src_ref=made_ref.at[0, 0],
            dst_ref=terms_ref.at[j, k],
            send_sem=send_sem.at[0, 0],
            recv_sem=recv_sem.at[j, k],
            device_id=worker_of(j, k, lat, lats, stride),
            device_id_type=MESH,
        ).wait_recv(),
        None,
    )


def transform(left, right, parts, pixels):
    low = jnp.bfloat16
    stacked = jnp.concatenate(
        [jnp.concatenate([p.astype(low) for p in pair], axis=0) for pair in parts], axis=1
    )
    dot = functools.partial(jnp.dot, preferred_element_type=jnp.float32)
    middle = (dot(left[0], stacked) + dot(left[1], stacked)).astype(low)
    rows = [
        jnp.concatenate(
            [
                middle[:pixels, m * pixels : (m + 1) * pixels],
                middle[pixels:, m * pixels : (m + 1) * pixels],
            ],
            axis=1,
        )
        for m in range(len(parts))
    ]
    joined = jnp.concatenate(rows, axis=0)
    ended = dot(joined, right[0]) + dot(joined, right[1])
    return [
        (
            ended[m * pixels : (m + 1) * pixels, :pixels],
            ended[m * pixels : (m + 1) * pixels, pixels:],
        )
        for m in range(len(parts))
    ]


def work_kernel(
    place_ref, held_ref, probe_ref, measured_ref, tables_ref, made_ref, saved, back
):
    sections, _, _, tile_rows, pixels = held_ref.shape
    modes = probe_ref.shape[0]
    keep = tile_rows - place_ref[2]

    def upper():
        return lax.broadcasted_iota(jnp.int32, (tile_rows, pixels), 0) < keep

    def patch(s):
        mask = upper()
        out = []
        for part in range(2):
            a, b, c = (held_ref[s, j, part].astype(jnp.float32) for j in range(TILES))
            out.append(
                jnp.concatenate([jnp.where(mask, a, b), jnp.where(mask, b, c)], axis=0)
            )
        return out

    @pl.when(place_ref[0] == 1)
    def _():
        saved[0] = probe_ref[...].astype(jnp.bfloat16)

        @pl.loop(0, sections)
        def _(s):
            p_real, p_imag = patch(s)
            lit = []
            for m in range(modes):
                w_real = saved[s, m, 0].astype(jnp.float32)
                w_imag = saved[s, m, 1].astype(jnp.float32)
                lit.append(
                    (p_real * w_real - p_imag * w_imag, p_real * w_imag + p_imag * w_real)
                )
            moved = transform(tables_ref[0], tables_ref[1], lit, pixels)
            for m in range(modes):
                for part in range(2):
                    saved[s + 1, m, part] = moved[m][part].astype(jnp.bfloat16)

        last = [(saved[sections, m, 0], saved[sections, m, 1]) for m in range(modes)]
        far = transform(tables_ref[2], tables_ref[3], last, pixels)
        resid = -measured_ref[place_ref[1]]
        for real, imag in far:
            resid = resid + (real * real + imag * imag)
        seed = [(resid * real, resid * imag) for real, imag in far]
        seed = transform(tables_ref[3], tables_ref[2], seed, pixels)
        for m in range(modes):
            for part in range(2):
                back[m, part] = seed[m][part].astype(jnp.bfloat16)

        @pl.loop(0, sections)
        def _(step):
            s = sections - 1 - step
            p_real, p_imag = patch(s)
            waves = [(back[m, 0], back[m, 1]) for m in range(modes)]
            lit = transform(tables_ref[1], tables_ref[0], waves, pixels)
            g_real = jnp.zeros((pixels, pixels), jnp.float32)
            g_imag = jnp.zeros((pixels, pixels), jnp.float32)
            for m in range(modes):
                l_real, l_imag = lit[m]
                w_real = saved[s, m, 0].astype(jnp.float32)
                w_imag = saved[s, m, 1].astype(jnp.float32)
                g_real = g_real + (w_real * l_real + w_imag * l_imag)
                g_imag = g_imag + (w_real * l_imag - w_imag * l_real)
                back[m, 0] = (p_real * l_real + p_imag * l_imag).astype(jnp.bfloat16)
                back[m, 1] = (p_real * l_imag - p_imag * l_real).astype(jnp.bfloat16)
            mask = upper()
            for part, term in enumerate((g_real, g_imag)):
                top, bottom = term[:tile_rows], term[tile_rows:]
                none = jnp.zeros_like(top)
                made_ref[s, 0, part] = jnp.where(mask, top, none).astype(made_ref.dtype)
                made_ref[s, 1, part] = jnp.where(mask, bottom, top).astype(made_ref.dtype)
                made_ref[s, 2, part] = jnp.where(mask, none, bottom).astype(made_ref.dtype)


def on_device(object_slices, probe, positions, measured):
    pixels = probe.shape[-1]
    modes = probe.shape[0]
    tile_rows, cols = object_slices.shape[2:]
    count = positions.shape[0]
    sections = lax.axis_size("depth")
    lats = lax.axis_size("lat")
    stride, me, lat, works = spread(count, sections, lats)
    window = jnp.minimum(me // stride, count - 1)
    low = jnp.bfloat16
    vmem = pl.BlockSpec(memory_space=pltpu.VMEM)
    smem = pl.BlockSpec(memory_space=pltpu.SMEM)
    anywhere = pl.BlockSpec(memory_space=pl.ANY)
    block = (2, tile_rows, pixels)
    local = pltpu.CompilerParams(vmem_limit_bytes=VMEM_BYTES)

    near = jnp.stack([positions] + [shifted(positions, "lat", j) for j in range(1, TILES)])
    own_row = lax.dynamic_index_in_dim(positions, window, 0, False)[0] % tile_rows
    place = jnp.stack([works.astype(jnp.int32), window, own_row]).astype(jnp.int32)

    blocks = pl.pallas_call(
        extract_kernel,
        out_shape=jax.ShapeDtypeStruct((TILES, count) + block, low),
        in_specs=[smem, vmem],
        out_specs=vmem,
        compiler_params=local,
        name="extract",
    )(near, object_slices[0])

    held = pl.pallas_call(
        functools.partial(scatter_kernel, count, sections, lats),
        out_shape=jax.ShapeDtypeStruct((sections, TILES) + block, low),
        in_specs=[anywhere],
        out_specs=anywhere,
        scratch_shapes=[
            pltpu.SemaphoreType.DMA((TILES, count)),
            pltpu.SemaphoreType.DMA((sections, TILES)),
            pltpu.SemaphoreType.DMA,
        ],
        compiler_params=pltpu.CompilerParams(collective_id=0, has_side_effects=True),
        name="scatter",
    )(blocks)

    made = pl.pallas_call(
        work_kernel,
        out_shape=jax.ShapeDtypeStruct((sections, TILES) + block, low),
        in_specs=[smem, vmem, vmem, vmem, vmem],
        out_specs=vmem,
        scratch_shapes=[
            pltpu.VMEM((sections + 1, modes, 2, pixels, pixels), low),
            pltpu.VMEM((modes, 2, pixels, pixels), low),
        ],
        compiler_params=local,
        name="work",
    )(place, held, probe, measured, host_tables(pixels))

    terms = pl.pallas_call(
        functools.partial(return_kernel, count, sections, lats),
        out_shape=jax.ShapeDtypeStruct((TILES, count) + block, low),
        in_specs=[anywhere],
        out_specs=anywhere,
        scratch_shapes=[
            pltpu.SemaphoreType.DMA((sections, TILES)),
            pltpu.SemaphoreType.DMA((TILES, count)),
            pltpu.SemaphoreType.DMA,
        ],
        compiler_params=pltpu.CompilerParams(collective_id=1, has_side_effects=True),
        name="give_back",
    )(made)

    total = pl.pallas_call(
        gather_kernel,
        out_shape=jax.ShapeDtypeStruct((2, tile_rows, cols), jnp.float32),
        in_specs=[smem, vmem],
        out_specs=vmem,
        compiler_params=local,
        name="gather",
    )(near, terms)
    return total[None]


def solution(mesh):
    return jax.shard_map(
        on_device,
        mesh=mesh,
        in_specs=(P("depth", None, "lat", None), P(), P("lat", None), P("lat", None, None)),
        out_specs=P("depth", None, "lat", None),
        check_vma=False,
    )
```

time: 804 us -> 129 us (0.16)
  the two profiles are of different devices: /device:TPU:0 before, /device:TPU:15 now
where the time goes in v1:
time: 129 us; the launch traced here: 128 us
  Pallas kernels  116 us (90%)
  local copies, waits for them, and re-layouts  8.02 us (6%)
  starting transfers between devices  2.03 us (2%)
  between operations  1.79 us (1%)
    pallas_call x1, Pallas kernels, on_device(): pl.pallas_call(functools.partial(return_kernel, count, sections, lats), o...  40.8 us
    pallas_call x1, Pallas kernels, on_device(): pl.pallas_call(functools.partial(scatter_kernel, count, sections, lats),...  39.7 us
    pallas_call x1, Pallas kernels, on_device(): pl.pallas_call(work_kernel, out_shape=jax.ShapeDtypeStruct((sections, TIL...  28.3 us
    unnamed x12, local copies, waits for them, and re-layouts  5.78 us
    pallas_call x1, Pallas kernels, on_device(): pl.pallas_call(gather_kernel, out_shape=jax.ShapeDtypeStruct((2, tile_row...  4.3 us
    pallas_call x1, Pallas kernels, on_device(): pl.pallas_call(extract_kernel, out_shape=jax.ShapeDtypeStruct((TILES, cou...  3.2 us
  transfers between devices with their start and end apart: 2, of which 0 were waited for; matrix products, arithmetic and copies ran while one was open for 2% of the time, Pallas kernels for 0%

profile of v1, /device:TPU:15, one launch (start us, length us, event | category | flops | bytes accessed | tf_op | source)
XLA Modules:
  0.0 128.3 jit_solution(16340714809956660603)
XLA Ops:
  0.0 0.8 collective-permute-start
  0.8 1.2 collective-permute-start.1
  2.0 0.8 constant_dynamic-slice_fusion
  2.8 0.5 slice.4
  5.0 0.8 copy.6
  5.8 0.1 pad_add_fusion.1.place_ref
  5.9 0.0 collective-permute-done
  5.9 0.1 copy.7
  6.0 0.0 collective-permute-done.1
  6.0 0.1 copy.8
  6.1 0.0 copy-start.3
  6.1 1.6 %copy-done.3 = f32[1,2,128,2048]{3,2,1,0:T(8,128)S(1)} copy-done((f32[1,2,128,2048]{3,2,1,0:T(8,128)S(1)}, f32[1,2,128,2048]{3,2,1,0:T(8,128)}, u32[]{:S(2)}) %copy-start.3) | copy-done | bytes 2097176
  7.7 3.2 %extract.1.blocks_ref = bf16[3,4,2,128,256]{4,3,2,1,0:T(8,128)(2,1)S(1)} custom-call(s32[3,4,2]{2,1,0:T(4,128)S(1)} %pad_add_fusion.positions_ref, f32[2,128,2048]{2,1,0:T(8,128)S(1)} %bitcast.9), custom_call_target="tpu_custom_call" | custom-call | tf_op jit(solution)/shard_map/extract/pallas_call | solution.py:362
  10.9 0.0 copy-start.2
  10.9 1.1 copy-done.2
  12.0 0.0 copy-start.4
  12.0 0.0 copy-start.5
  12.0 39.7 %scatter.1.held_ref = bf16[8,3,2,128,256]{4,3,2,1,0:T(8,128)(2,1)} custom-call(bf16[3,4,2,128,256]{4,3,2,1,0:T(8,128)(2,1)} %copy-done.2), custom_call_target="tpu_custom_call" | custom-call | tf_op jit(solution)/shard_map/scatter/pallas_call | solution.py:371
  51.7 0.0 copy-done.4
  51.7 0.0 copy-done.5
  51.8 28.3 %work.1.made_ref = bf16[8,3,2,128,256]{4,3,2,1,0:T(8,128)(2,1)S(1)} custom-call(s32[3]{0:T(128)S(1)} %pad_add_fusion.1.place_ref, bf16[8,3,2,128,256]{4,3,2,1,0:T(8,128)(2,1)} %scatter.1.held_ref, f32[2,2,256,256]{3,2,1,0:T(8,128)S(1)} %copy-done.4, f32[4,256,256]{2,1,0:T(8,128)S(1)} %copy-done.5, bf16[4,2,512,512]{3,2,1,0:T(8,128)(2,1)} %constant.49.clone.tables_ref), custom_call_target="tpu_custom_call" | custom-call | tf_op jit(solution)/shard_map/work/pallas_call | solution.py:385
  80.1 0.0 copy-start
  80.1 1.6 %copy-done = bf16[8,3,2,128,256]{4,3,2,1,0:T(8,128)(2,1)} copy-done((bf16[8,3,2,128,256]{4,3,2,1,0:T(8,128)(2,1)}, bf16[8,3,2,128,256]{4,3,2,1,0:T(8,128)(2,1)S(1)}, u32[]{:S(2)}) %copy-start) | copy-done | bytes 3145752
  81.7 40.8 %give_back.1.terms_ref = bf16[3,4,2,128,256]{4,3,2,1,0:T(8,128)(2,1)} custom-call(bf16[8,3,2,128,256]{4,3,2,1,0:T(8,128)(2,1)} %copy-done), custom_call_target="tpu_custom_call" | custom-call | tf_op jit(solution)/shard_map/give_back/pallas_call | solution.py:398
  122.6 0.0 copy-start.1
  122.6 1.4 %copy-done.1 = bf16[3,4,2,128,256]{4,3,2,1,0:T(8,128)(2,1)S(1)} copy-done((bf16[3,4,2,128,256]{4,3,2,1,0:T(8,128)(2,1)S(1)}, bf16[3,4,2,128,256]{4,3,2,1,0:T(8,128)(2,1)}, u32[]{:S(2)}) %copy-start.1) | copy-done | bytes 1572888
  124.0 4.3 %gather.1 = f32[2,128,2048]{2,1,0:T(8,128)} custom-call(s32[3,4,2]{2,1,0:T(4,128)S(1)} %pad_add_fusion.positions_ref, bf16[3,4,2,128,256]{4,3,2,1,0:T(8,128)(2,1)S(1)} %copy-done.1), custom_call_target="tpu_custom_call" | custom-call | tf_op jit(solution)/shard_map/gather/pallas_call | solution.py:412
  (1 shorter events, 0.0 us)
Async XLA Ops:
  0.0 5.9 %collective-permute-start = (s32[4,2]{0,1:T(2,128)}, s32[4,2]{0,1:T(2,128)S(1)}, u32[]{:S(2)}, u32[]{:S(2)}) collective-permute-start(s32[4,2]{0,1:T(2,128)} %param.7), channel_id=1, source_target_pairs={{3,0},{0,1},{1,2},{2,3},{7,4},{4,5},{5,6},{6,7},{11,8},{8,9},{9,10... | collective-permute-start | bytes 104 | tf_op jit(solution)/shard_map/ppermute | solution.py:23
  0.8 5.2 %collective-permute-start.1 = (s32[4,2]{0,1:T(2,128)}, s32[4,2]{0,1:T(2,128)S(1)}, u32[]{:S(2)}, u32[]{:S(2)}) collective-permute-start(s32[4,2]{0,1:T(2,128)} %param.7), channel_id=1, source_target_pairs={{2,0},{3,1},{0,2},{1,3},{6,4},{7,5},{4,6},{5,7},{10,8},{11,9},{8,1... | collective-permute-start | bytes 104 | tf_op jit(solution)/shard_map/ppermute | solution.py:23
  6.1 1.6 %copy-start.3 = (f32[1,2,128,2048]{3,2,1,0:T(8,128)S(1)}, f32[1,2,128,2048]{3,2,1,0:T(8,128)}, u32[]{:S(2)}) copy-start(f32[1,2,128,2048]{3,2,1,0:T(8,128)} %param.5) | copy-start | bytes 6291460
  10.9 1.1 copy-start.2
  12.0 39.7 %copy-start.4 = (f32[2,2,256,256]{3,2,1,0:T(8,128)S(1)}, f32[2,2,256,256]{3,2,1,0:T(8,128)}, u32[]{:S(2)}) copy-start(f32[2,2,256,256]{3,2,1,0:T(8,128)} %probe_ref.1) | copy-start | bytes 3145732
  12.0 39.7 %copy-start.5 = (f32[4,256,256]{2,1,0:T(8,128)S(1)}, f32[4,256,256]{2,1,0:T(8,128)}, u32[]{:S(2)}) copy-start(f32[4,256,256]{2,1,0:T(8,128)} %measured_ref.1) | copy-start | bytes 3145732
  80.1 1.6 %copy-start = (bf16[8,3,2,128,256]{4,3,2,1,0:T(8,128)(2,1)}, bf16[8,3,2,128,256]{4,3,2,1,0:T(8,128)(2,1)S(1)}, u32[]{:S(2)}) copy-start(bf16[8,3,2,128,256]{4,3,2,1,0:T(8,128)(2,1)S(1)} %work.1.made_ref) | copy-start | bytes 9437188
  122.6 1.4 %copy-start.1 = (bf16[3,4,2,128,256]{4,3,2,1,0:T(8,128)(2,1)S(1)}, bf16[3,4,2,128,256]{4,3,2,1,0:T(8,128)(2,1)}, u32[]{:S(2)}) copy-start(bf16[3,4,2,128,256]{4,3,2,1,0:T(8,128)(2,1)} %give_back.1.terms_ref) | copy-start | bytes 4718596
